TPU v7x, 32 devices: a whole 2x2x4 slice. The times are simulated.
32 devices in a mesh: section: 4 (over x, core), tp: 8 (over z, y).
Axes of the slice: x: 2, y: 2, z: 4, core: 2. Of those that a mesh axis runs over, the one named last changes fastest.
Arguments:
- grad_attn: bfloat16 [4, 8, 128, 128], P('section', 'tp'), may hold values from -6 to 6
- w_value: bfloat16 [4, 12288, 1024], P('section', 'tp'), may hold values from -0.0546875 to 0.0546875
- probs_own: bfloat16 [4, 8, 128, 128], P('section', 'tp'), may hold values from 0.0009994507 to 0.25
- probs_spare: bfloat16 [4, 8, 128, 128], P('section', 'tp'), may hold values from 0.0009994507 to 0.25
- evicted: int32 [4, 4], P('section'), may hold values from 0 to 1, as said below
- layer_input: bfloat16 [4, 128, 12288], P('section', None, 'tp'), may hold values from -6 to 6
- gain: float32 [4, 12288], P('section', 'tp'), may hold values from 0.1 to 1.9
Outputs:
- handed: bfloat16 [4, 128, 12288], P('section', None, 'tp')
Inputs may be any that keep to these rules, and one draw needn't show every extreme that they name: Section 0 has every tile evicted.
All inputs are finite; a program needn't handle non-finite values.
Results may differ from a plain program's by a relative error of at most 0.0049.
Values may be sent and summed in bfloat16 or wider, within the bound.
No kernel may reach another device: no remote copies, remote signals or barrier semaphores. Data moves between devices by JAX's collectives and lax.ppermute only.
A program may use at most 64 MiB of HBM per device.

v0:
```python
import jax
import jax.numpy as jnp
from jax import lax
from jax.sharding import PartitionSpec as P

D = 12288


def passed_along(block, axis, distance):
    devices = range(lax.axis_size(axis))
    route = [((i - distance) % len(devices), i) for i in devices]
    return lax.ppermute(block, axis, route)


def per_device(grad_attn, w_value, probs_own, probs_spare, evicted, layer_input, gain):
    sections = lax.axis_size("section")
    fetched = probs_spare
    fetched = passed_along(fetched, "section", sections // 2)
    tokens = probs_own.shape[2]
    head_size = grad_attn.shape[3]
    flags = jnp.repeat(evicted[0], tokens // evicted.shape[1])
    mixed = jnp.where(flags[None, :, None] == 1, fetched[0], probs_own[0])
    weights = w_value[0]
    features = weights.shape[0]
    values = layer_input[0].astype(jnp.float32)
    scales = gain[0]
    squares = lax.psum(jnp.sum(values * values, axis=1), "tp")
    grad_value = jnp.einsum(
        "hqk,hqd->hkd", mixed, grad_attn[0], preferred_element_type=jnp.float32
    ).astype(jnp.bfloat16)
    grads = lax.all_gather(grad_value, "tp", axis=0, tiled=True)
    count = grads.shape[0]
    columns = weights
    columns = columns.reshape(features, count, head_size)
    grad_normed = jnp.einsum("hkd,fhd->kf", grads, columns, preferred_element_type=jnp.float32)
    local_inner = jnp.sum(scales[None, :] * grad_normed * values, axis=1)
    inner = lax.psum(local_inner, "tp")
    inv = 1.0 / jnp.sqrt(squares / D + 1e-05)
    branch = scales[None, :] * grad_normed * inv[:, None] - values * (inner * inv**3 / D)[:, None]
    branch = branch.astype(jnp.bfloat16)[None]
    return passed_along(branch, "section", -1)


def solution(mesh):
    in_specs = (
        P("section", "tp", None, None),
        P("section", "tp", None),
        P("section", "tp", None, None),
        P("section", "tp", None, None),
        P("section", None),
        P("section", None, "tp"),
        P("section", "tp"),
    )
    out_specs = P("section", None, "tp")
    return jax.shard_map(
        per_device, mesh=mesh, in_specs=in_specs, out_specs=out_specs, check_vma=False
    )
```

profile of v0, /device:TPU:1, one launch (start us, length us, event | category | flops | bytes accessed | tf_op | source)
XLA Modules:
  0.0 70.2 jit_solution(14645517707696060295)
XLA Ops:
  0.0 0.0 copy-start
  0.0 2.0 %collective-permute-start = (bf16[1,1,128,128]{3,2,1,0:T(8,128)(2,1)}, bf16[1,1,128,128]{3,2,1,0:T(8,128)(2,1)S(1)}, u32[]{:S(2)}, u32[]{:S(2)}) collective-permute-start(bf16[1,1,128,128]{3,2,1,0:T(8,128)(2,1)} %param.10), channel_id=1, source_target_pairs={{16,0},{24,8},{0,16},{8,24},{17,1},{25,9},{1,17},{9,25},{18,2},{26... | collective-permute-start | bytes 98312 | tf_op jit(solution)/shard_map/ppermute | solution.py:12
  2.0 0.7 compare_bitcast_fusion
  2.7 0.1 broadcast_in_dim.16
  2.8 0.1 eq.21
  2.9 0.0 copy-start.2
  2.9 0.0 copy-start.1
  2.9 2.7 %copy.9 = bf16[192,8,8,128]{3,2,1,0:T(8,128)(2,1)S(1)} copy(bf16[192,8,8,128]{3,1,2,0:T(8,128)(2,1)} %bitcast.34) | data formatting | bytes 6291456
  5.6 0.0 copy-done.2
  5.6 0.0 collective-permute-done
  5.6 0.0 copy-done
  5.7 0.0 copy-done.1
  5.7 0.3 convolution_convert_fusion
  5.9 24.7 %all-gather = bf16[1024,128]{1,0:T(8,128)(2,1)S(1)} all-gather(bf16[128,128]{1,0:T(8,128)(2,1)S(1)} %convolution_convert_fusion), channel_id=2, replica_groups=mesh['section'=4,'tp'=8] {'tp'}, dimensions={0}, use_global_device_ids=true | all-gather | bytes 294912 | tf_op jit(solution)/shard_map/all_gather | solution.py:31
  30.6 3.1 %fusion.8 = (f32[128]{0:T(128)S(1)}, f32[128]{0:T(128)S(1)}, f32[128,1536]{1,0:T(8,128)}) fusion(bf16[1,128,1536]{2,1,0:T(8,128)(2,1)} %param.12, bf16[8,128,128]{2,1,0:T(8,128)(2,1)S(1)} %bitcast.36, bf16[1536,8,128]{2,1,0:T(8,128)(2,1)S(1)} %bitcast.35, f32[1536]{0:T(1024)S(1)} %reduce), kind=kOutput, calls=%fused_computation.8 | convolution fusion | flops 403832576 | bytes 4594688 | tf_op jit(solution)/shard_map/hkd,fhd->kf/dot_general | solution.py:35
  33.7 18.0 %all-reduce = (f32[128]{0:T(128)S(1)}, f32[128]{0:T(128)S(1)}) all-reduce(f32[128]{0:T(128)S(1)} %get-tuple-element.6, f32[128]{0:T(128)S(1)} %get-tuple-element.5), channel_id=1, replica_groups=mesh['section'=4,'tp'=8] {'tp'}, use_global_device_ids=true, to_apply=%region_3.4 | all-reduce | flops 256 | bytes 2048 | tf_op jit(solution)/shard_map/psum | solution.py:37
  51.7 1.4 %fusion.12 = bf16[1,128,1536]{2,1,0:T(8,128)(2,1)S(1)} fusion(f32[128,1536]{1,0:T(8,128)} %get-tuple-element.11, bf16[1,128,1536]{2,1,0:T(8,128)(2,1)} %param.12, f32[128]{0:T(128)S(1)} %get-tuple-element.10, f32[128]{0:T(128)S(1)} %get-tuple-element.9), kind=kLoop, calls=%fused_computation.12 | loop fusion | flops 983040 | bytes 1573888 | tf_op jit(solution)/shard_map/broadcast_in_dim | solution.py:40
  53.2 10.7 %collective-permute-start.1 = (bf16[1,128,1536]{2,1,0:T(8,128)(2,1)S(1)}, bf16[1,128,1536]{2,1,0:T(8,128)(2,1)S(1)}, u32[]{:S(2)}, u32[]{:S(2)}) collective-permute-start(bf16[1,128,1536]{2,1,0:T(8,128)(2,1)S(1)} %fusion.12), channel_id=1, source_target_pairs={{8,0},{16,8},{24,16},{0,24},{9,1},{17,9},{25,17},{1,25},{10,2},{18... | collective-permute-start | bytes 1179656 | tf_op jit(solution)/shard_map/ppermute | solution.py:12
  63.8 5.6 %collective-permute-done.1 = bf16[1,128,1536]{2,1,0:T(8,128)(2,1)S(1)} collective-permute-done((bf16[1,128,1536]{2,1,0:T(8,128)(2,1)S(1)}, bf16[1,128,1536]{2,1,0:T(8,128)(2,1)S(1)}, u32[]{:S(2)}, u32[]{:S(2)}) %collective-permute-start.1) | collective-permute-done | bytes 393248 | tf_op jit(solution)/shard_map/ppermute | solution.py:12
  69.4 0.7 %copy.19 = bf16[1,128,1536]{2,1,0:T(8,128)(2,1)} copy(bf16[1,128,1536]{2,1,0:T(8,128)(2,1)S(1)} %collective-permute-done.1) | data formatting | bytes 786432
  (2 shorter events, 0.0 us)
Async XLA Ops:
  0.0 5.6 %copy-start = (bf16[1,1,128,128]{3,2,1,0:T(8,128)(2,1)S(1)}, bf16[1,1,128,128]{3,2,1,0:T(8,128)(2,1)}, u32[]{:S(2)}) copy-start(bf16[1,1,128,128]{3,2,1,0:T(8,128)(2,1)} %param.7) | copy-start | bytes 98308
  0.0 5.6 %collective-permute-start = (bf16[1,1,128,128]{3,2,1,0:T(8,128)(2,1)}, bf16[1,1,128,128]{3,2,1,0:T(8,128)(2,1)S(1)}, u32[]{:S(2)}, u32[]{:S(2)}) collective-permute-start(bf16[1,1,128,128]{3,2,1,0:T(8,128)(2,1)} %param.10), channel_id=1, source_target_pairs={{16,0},{24,8},{0,16},{8,24},{17,1},{25,9},{1,17},{9,25},{18,2},{26... | collective-permute-start | bytes 98312 | tf_op jit(solution)/shard_map/ppermute | solution.py:12
  2.9 2.7 %copy-start.2 = (f32[1,1536]{1,0:T(1,128)S(1)}, f32[1,1536]{1,0:T(1,128)}, u32[]{:S(2)}) copy-start(f32[1,1536]{1,0:T(1,128)} %param.13) | copy-start | bytes 18436
  2.9 2.8 %copy-start.1 = (bf16[1,1,128,128]{3,2,1,0:T(8,128)(2,1)S(1)}, bf16[1,1,128,128]{3,2,1,0:T(8,128)(2,1)}, u32[]{:S(2)}) copy-start(bf16[1,1,128,128]{3,2,1,0:T(8,128)(2,1)} %param.9) | copy-start | bytes 98308
  53.2 16.3 %collective-permute-start.1 = (bf16[1,128,1536]{2,1,0:T(8,128)(2,1)S(1)}, bf16[1,128,1536]{2,1,0:T(8,128)(2,1)S(1)}, u32[]{:S(2)}, u32[]{:S(2)}) collective-permute-start(bf16[1,128,1536]{2,1,0:T(8,128)(2,1)S(1)} %fusion.12), channel_id=1, source_target_pairs={{8,0},{16,8},{24,16},{0,24},{9,1},{17,9},{25,17},{1,25},{10,2},{18... | collective-permute-start | bytes 1179656 | tf_op jit(solution)/shard_map/ppermute | solution.py:12
where the time goes:
time: 70.4 us; the launch traced here: 70.2 us
  blocking collectives  42.7 us (61%)
  starting transfers between devices  12.7 us (18%)
  waiting for transfers between devices  5.6 us (8%)
  local copies, waits for them, and re-layouts  3.64 us (5%)
  matrix products  3.32 us (5%)
  other arithmetic  2.11 us (3%)
    all_gather x1, blocking collectives, per_device(): grads = lax.all_gather(grad_value, 'tp', axis=0, tiled=True)  24.7 us
    psum x1, blocking collectives, per_device(): inner = lax.psum(local_inner, 'tp')  18 us
    ppermute x2, starting transfers between devices, passed_along(): return lax.ppermute(block, axis, route)  12.7 us
    ppermute x2, waiting for transfers between devices, passed_along(): return lax.ppermute(block, axis, route)  5.6 us
    unnamed x8, local copies, waits for them, and re-layouts  3.47 us
    dot_general x1, matrix products, per_device(): jnp.einsum('hkd,fhd->kf', grads, columns, preferred_element_type=jnp.floa...  3.06 us
    broadcast_in_dim x1, other arithmetic, per_device(): branch = branch.astype(jnp.bfloat16)[None]  1.42 us
  transfers between devices with their start and end apart: 2, of which 1 were waited for; matrix products, arithmetic and copies ran while one was open for 5% of the time, Pallas kernels for 0%

commit v1 on v0

v1 whole, which is shorter than its diff:
```python
import jax
import jax.numpy as jnp
from jax import lax
from jax.sharding import PartitionSpec as P

D = 12288


def passed_along(block, axis, distance):
    devices = range(lax.axis_size(axis))
    route = [((i - distance) % len(devices), i) for i in devices]
    return lax.ppermute(block, axis, route)


def summed_over(block, axis):
    total = block
    for distance in range(1, lax.axis_size(axis)):
        total = total + passed_along(block, axis, distance)
    return total


def per_device(grad_attn, w_value, probs_own, probs_spare, evicted, layer_input, gain):
    sections = lax.axis_size("section")
    count = lax.axis_size("tp")
    fetched = passed_along(probs_spare, "section", sections // 2)
    tokens = probs_own.shape[2]
    head_size = grad_attn.shape[3]
    flags = jnp.repeat(evicted[0], tokens // evicted.shape[1])
    mixed = jnp.where(flags[None, :, None] == 1, fetched[0], probs_own[0])
    values = layer_input[0].astype(jnp.float32)
    scales = gain[0]
    grad_value = jnp.einsum(
        "qk,qd->kd", mixed[0], grad_attn[0, 0], preferred_element_type=jnp.float32
    ).astype(jnp.bfloat16)
    copies = jnp.broadcast_to(grad_value[None], (count, tokens, head_size))
    grads = lax.all_to_all(copies, "tp", 0, 0, tiled=True)
    flat = jnp.transpose(grads, (1, 0, 2)).reshape(tokens, count * head_size)
    grad_normed = lax.dot_general(
        flat, w_value[0], (((1,), (1,)), ((), ())), preferred_element_type=jnp.float32
    )
    scaled = scales[None, :] * grad_normed
    sums = jnp.stack([jnp.sum(values * values, axis=1), jnp.sum(scaled * values, axis=1)])
    squares, inner = summed_over(sums, "tp")
    inv = 1.0 / jnp.sqrt(squares / D + 1e-05)
    branch = scaled * inv[:, None] - values * (inner * inv**3 / D)[:, None]
    branch = branch.astype(jnp.bfloat16)[None]
    return passed_along(branch, "section", -1)


def solution(mesh):
    in_specs = (
        P("section", "tp", None, None),
        P("section", "tp", None),
        P("section", "tp", None, None),
        P("section", "tp", None, None),
        P("section", None),
        P("section", None, "tp"),
        P("section", "tp"),
    )
    out_specs = P("section", None, "tp")
    return jax.shard_map(
        per_device, mesh=mesh, in_specs=in_specs, out_specs=out_specs, check_vma=False
    )
```

time: 70.4 us -> 51.3 us (0.73)
  blocking collectives: 42.7 us -> 0 us
  waiting for transfers between devices: 5.6 us -> 19 us
  starting transfers between devices: 12.7 us -> 22.3 us
    all_gather x1 -> x0, blocking collectives: 24.7 us -> none  [per_device(): grads = lax.all_gather(grad_value, 'tp', axis=0, tiled=True)]
    psum x1 -> x0, blocking collectives: 18 us -> none  [per_device(): inner = lax.psum(local_inner, 'tp')]
    ppermute x2 -> x9, waiting for transfers between devices: 5.6 us -> 12.5 us  [passed_along(): return lax.ppermute(block, axis, route)]
    all_to_all x0 -> x1, waiting for transfers between devices: none -> 6.51 us  [per_device(): grads = lax.all_to_all(copies, 'tp', 0, 0, tiled=True)]
    all_to_all x0 -> x1, starting transfers between devices: none -> 5.81 us  [per_device(): grads = lax.all_to_all(copies, 'tp', 0, 0, tiled=True)]
    ppermute x2 -> x9, starting transfers between devices: 12.7 us -> 16.5 us  [passed_along(): return lax.ppermute(block, axis, route)]
    unnamed x8 -> x5, local copies, waits for them, and re-layouts: 3.47 us -> 0.75 us
    broadcast_in_dim x0 -> x1, local copies, waits for them, and re-layouts: none -> 1.49 us  [per_device(): copies = jnp.broadcast_to(grad_value[None], (count, tokens, head_size))]
  transfers between devices with their start and end apart: 2 -> 10, of which waited for: 1 -> 5; matrix products, arithmetic and copies ran while one was open for 5% -> 3% of each run, Pallas kernels for 0% -> 0%
where the time goes in v1:
time: 51.3 us; the launch traced here: 50.8 us
  starting transfers between devices  22.3 us (43%)
  waiting for transfers between devices  19 us (37%)
  matrix products  4 us (8%)
  local copies, waits for them, and re-layouts  3.87 us (8%)
  other arithmetic  1.6 us (3%)
    ppermute x9, starting transfers between devices, passed_along(): return lax.ppermute(block, axis, route)  16.5 us
    ppermute x9, waiting for transfers between devices, passed_along(): return lax.ppermute(block, axis, route)  12.5 us
    all_to_all x1, waiting for transfers between devices, per_device(): grads = lax.all_to_all(copies, 'tp', 0, 0, tiled=True)  6.51 us
    all_to_all x1, starting transfers between devices, per_device(): grads = lax.all_to_all(copies, 'tp', 0, 0, tiled=True)  5.81 us
    dot_general x1, matrix products, per_device(): lax.dot_general(flat, w_value[0], (((1,), (1,)), ((), ())), preferred_ele...  2.34 us
    dot_general x1, matrix products, per_device(): jnp.einsum('qk,qd->kd', mixed[0], grad_attn[0, 0], preferred_element_type...  1.66 us
    broadcast_in_dim x1, local copies, waits for them, and re-layouts, per_device(): copies = jnp.broadcast_to(grad_value[None], (count, tokens, head_size))  1.49 us
    convert_element_type x1, local copies, waits for them, and re-layouts, per_device(): grad_value = jnp.einsum('qk,qd->kd', mixed[0], grad_attn[0, 0], preferred...  1.46 us
  transfers between devices with their start and end apart: 10, of which 5 were waited for; matrix products, arithmetic and copies ran while one was open for 3% of the time, Pallas kernels for 0%

profile of v1, /device:TPU:1, one launch (start us, length us, event | category | flops | bytes accessed | tf_op | source)
XLA Modules:
  0.0 50.8 jit_solution(11051989651652042051)
XLA Ops:
  0.0 0.0 copy-start
  0.0 0.0 copy-start.1
  0.0 2.0 %collective-permute-start = (bf16[1,1,128,128]{3,2,1,0:T(8,128)(2,1)}, bf16[1,1,128,128]{3,2,1,0:T(8,128)(2,1)}, u32[]{:S(2)}, u32[]{:S(2)}) collective-permute-start(bf16[1,1,128,128]{3,2,1,0:T(8,128)(2,1)} %param.10), channel_id=1, source_target_pairs={{16,0},{24,8},{0,16},{8,24},{17,1},{25,9},{1,17},{9,25},{18,2},{26... | collective-permute-start | bytes 98312 | tf_op jit(solution)/shard_map/ppermute | solution.py:12
  2.0 0.7 %compare_bitcast_fusion = pred[4]{0:T(512)(128)(4,1)S(1)} fusion(s32[1,4]{1,0:T(1,128)} %param.11), kind=kLoop, calls=%fused_computation.17 | loop fusion | flops 4 | bytes 20 | tf_op jit(solution)/shard_map/eq | solution.py:29
  2.7 0.1 broadcast_in_dim.22
  2.8 0.1 eq.21
  2.9 0.8 %collective-permute-done = bf16[1,1,128,128]{3,2,1,0:T(8,128)(2,1)} collective-permute-done((bf16[1,1,128,128]{3,2,1,0:T(8,128)(2,1)}, bf16[1,1,128,128]{3,2,1,0:T(8,128)(2,1)}, u32[]{:S(2)}, u32[]{:S(2)}) %collective-permute-start) | collective-permute-done | bytes 32800 | tf_op jit(solution)/shard_map/ppermute | solution.py:12
  3.7 1.7 %convolution_convert_fusion = bf16[128,128]{1,0:T(8,128)(2,1)} fusion(bf16[1,1,128,128]{3,2,1,0:T(8,128)(2,1)} %param.7, bf16[1,1,128,128]{3,2,1,0:T(8,128)(2,1)} %param.9, bf16[1,1,128,128]{3,2,1,0:T(8,128)(2,1)} %collective-permute-done, pred[128]{0:T(512)(128)(4,1)S(1)} %eq.21), kind=kOutput, calls=%fused_computation.6 | convolution fusion | flops 4227072 | bytes 131200 | tf_op jit(solution)/shard_map/qk,qd->kd/dot_general | solution.py:32
  5.3 1.5 %copy.8 = bf16[128,128]{0,1:T(8,128)(2,1)} copy(bf16[128,128]{1,0:T(8,128)(2,1)} %convolution_convert_fusion) | data formatting | bytes 65536 | tf_op jit(solution)/shard_map/convert_element_type | solution.py:34
  6.8 1.5 %broadcast_in_dim.24 = bf16[8,128,128]{1,2,0:T(8,128)(2,1)} broadcast(bf16[128,128]{0,1:T(8,128)(2,1)} %copy.8), dimensions={1,2} | broadcast | bytes 294912 | tf_op jit(solution)/shard_map/broadcast_in_dim | solution.py:35
  8.3 5.8 %all-to-all-start = ((bf16[8,128,128]{1,2,0:T(8,128)(2,1)}), bf16[8,128,128]{1,2,0:T(8,128)(2,1)}, u32[]{:S(2)}, u32[]{:S(2)}) async-start(bf16[8,128,128]{1,2,0:T(8,128)(2,1)} %broadcast_in_dim.24), calls=%async_computation | async-start | bytes 524288 | tf_op jit(solution)/shard_map/all_to_all | solution.py:36
  14.1 0.7 %reduce = f32[1536]{0:T(1024)S(1)} reduce(f32[1,1536]{1,0:T(1,128)} %param.13, f32[]{:T(128)} %constant.18), dimensions={0}, to_apply=%param.13.reduce_sub_computation | reduce | bytes 12292 | tf_op args[6]
  14.8 6.5 %all-to-all-done = bf16[8,128,128]{1,2,0:T(8,128)(2,1)} async-done(((bf16[8,128,128]{1,2,0:T(8,128)(2,1)}), bf16[8,128,128]{1,2,0:T(8,128)(2,1)}, u32[]{:S(2)}, u32[]{:S(2)}) %all-to-all-start) | async-done | bytes 262176 | tf_op jit(solution)/shard_map/all_to_all | solution.py:36
  21.3 0.0 copy-done
  21.3 2.3 %fusion.5 = (f32[128]{0:T(128)S(1)}, f32[128]{0:T(128)S(1)}, f32[128,1536]{1,0:T(8,128)S(1)}) fusion(bf16[1,128,1536]{2,1,0:T(8,128)(2,1)} %param.12, bf16[128,1024]{0,1:T(8,128)(2,1)} %bitcast.6, bf16[1,1536,1024]{2,1,0:T(8,128)(2,1)S(1)} %copy-done, f32[1536]{0:T(1024)S(1)} %reduce), kind=kOutput, calls=%fused_computation.7 | convolution fusion | flops 403832576 | bytes 4594688 | tf_op jit(solution)/shard_map/dot_general | solution.py:38
  23.7 2.1 %collective-permute-start.6 = (f32[2,128]{1,0:T(2,128)S(1)}, f32[2,128]{1,0:T(2,128)S(1)}, u32[]{:S(2)}, u32[]{:S(2)}) collective-permute-start(f32[2,128]{1,0:T(2,128)S(1)} %pad_maximum_fusion), channel_id=1, source_target_pairs={{2,0},{3,1},{4,2},{5,3},{6,4},{7,5},{0,6},{1,7},{10,8},{11,9},{12,... | collective-permute-start | bytes 3080 | tf_op jit(solution)/shard_map/ppermute | solution.py:12
  25.8 0.0 collective-permute-start.5
  25.8 2.8 %collective-permute-start.4 = (f32[2,128]{1,0:T(2,128)S(1)}, f32[2,128]{1,0:T(2,128)S(1)}, u32[]{:S(2)}, u32[]{:S(2)}) collective-permute-start(f32[2,128]{1,0:T(2,128)S(1)} %pad_maximum_fusion), channel_id=1, source_target_pairs={{4,0},{5,1},{6,2},{7,3},{0,4},{1,5},{2,6},{3,7},{12,8},{13,9},{14,... | collective-permute-start | bytes 3080 | tf_op jit(solution)/shard_map/ppermute | solution.py:12
  28.6 0.0 collective-permute-start.3
  28.6 0.8 %collective-permute-start.2 = (f32[2,128]{1,0:T(2,128)S(1)}, f32[2,128]{1,0:T(2,128)S(1)}, u32[]{:S(2)}, u32[]{:S(2)}) collective-permute-start(f32[2,128]{1,0:T(2,128)S(1)} %pad_maximum_fusion), channel_id=1, source_target_pairs={{6,0},{7,1},{0,2},{1,3},{2,4},{3,5},{4,6},{5,7},{14,8},{15,9},{8,1... | collective-permute-start | bytes 3080 | tf_op jit(solution)/shard_map/ppermute | solution.py:12
  29.4 0.0 collective-permute-done.6
  29.4 3.4 %collective-permute-start.7 = (f32[2,128]{1,0:T(2,128)S(1)}, f32[2,128]{1,0:T(2,128)S(1)}, u32[]{:S(2)}, u32[]{:S(2)}) collective-permute-start(f32[2,128]{1,0:T(2,128)S(1)} %pad_maximum_fusion), channel_id=1, source_target_pairs={{1,0},{2,1},{3,2},{4,3},{5,4},{6,5},{7,6},{0,7},{9,8},{10,9},{11,1... | collective-permute-start | bytes 3080 | tf_op jit(solution)/shard_map/ppermute | solution.py:12
  32.8 0.0 collective-permute-done.5
  32.8 0.0 collective-permute-start.1
  32.8 0.0 collective-permute-done.4
  32.8 0.0 collective-permute-done.3
  32.8 0.0 collective-permute-done.2
  32.8 0.7 %collective-permute-done.7 = f32[2,128]{1,0:T(2,128)S(1)} collective-permute-done((f32[2,128]{1,0:T(2,128)S(1)}, f32[2,128]{1,0:T(2,128)S(1)}, u32[]{:S(2)}, u32[]{:S(2)}) %collective-permute-start.7) | collective-permute-done | bytes 1056 | tf_op jit(solution)/shard_map/ppermute | solution.py:12
  33.5 4.4 %collective-permute-done.1 = f32[2,128]{1,0:T(2,128)S(1)} collective-permute-done((f32[2,128]{1,0:T(2,128)S(1)}, f32[2,128]{1,0:T(2,128)S(1)}, u32[]{:S(2)}, u32[]{:S(2)}) %collective-permute-start.1) | collective-permute-done | bytes 1056 | tf_op jit(solution)/shard_map/ppermute | solution.py:12
  37.9 0.0 copy-done.1
  37.9 0.2 fusion.9
  38.1 5.4 %collective-permute-start.8 = (bf16[1,128,1536]{2,1,0:T(8,128)(2,1)S(1)}, bf16[1,128,1536]{2,1,0:T(8,128)(2,1)S(1)}, u32[]{:S(2)}, u32[]{:S(2)}) collective-permute-start(bf16[1,128,1536]{2,1,0:T(8,128)(2,1)S(1)} %fusion.9), channel_id=1, source_target_pairs={{8,0},{16,8},{24,16},{0,24},{9,1},{17,9},{25,17},{1,25},{10,2},{18... | collective-permute-start | bytes 1179656 | tf_op jit(solution)/shard_map/ppermute | solution.py:12
  43.5 6.6 %collective-permute-done.8 = bf16[1,128,1536]{2,1,0:T(8,128)(2,1)S(1)} collective-permute-done((bf16[1,128,1536]{2,1,0:T(8,128)(2,1)S(1)}, bf16[1,128,1536]{2,1,0:T(8,128)(2,1)S(1)}, u32[]{:S(2)}, u32[]{:S(2)}) %collective-permute-start.8) | collective-permute-done | bytes 393248 | tf_op jit(solution)/shard_map/ppermute | solution.py:12
  50.1 0.7 %copy.10 = bf16[1,128,1536]{2,1,0:T(8,128)(2,1)} copy(bf16[1,128,1536]{2,1,0:T(8,128)(2,1)S(1)} %collective-permute-done.8) | data formatting | bytes 786432
  (4 shorter events, 0.0 us)
Async XLA Ops:
  0.0 21.3 %copy-start = (bf16[1,1536,1024]{2,1,0:T(8,128)(2,1)S(1)}, bf16[1,1536,1024]{2,1,0:T(8,128)(2,1)}, u32[]{:S(2)}) copy-start(bf16[1,1536,1024]{2,1,0:T(8,128)(2,1)} %param.8) | copy-start | bytes 9437188
  0.0 37.9 %copy-start.1 = (bf16[1,128,1536]{2,1,0:T(8,128)(2,1)S(1)}, bf16[1,128,1536]{2,1,0:T(8,128)(2,1)}, u32[]{:S(2)}) copy-start(bf16[1,128,1536]{2,1,0:T(8,128)(2,1)} %param.12) | copy-start | bytes 1179652
  0.0 3.7 %collective-permute-start = (bf16[1,1,128,128]{3,2,1,0:T(8,128)(2,1)}, bf16[1,1,128,128]{3,2,1,0:T(8,128)(2,1)}, u32[]{:S(2)}, u32[]{:S(2)}) collective-permute-start(bf16[1,1,128,128]{3,2,1,0:T(8,128)(2,1)} %param.10), channel_id=1, source_target_pairs={{16,0},{24,8},{0,16},{8,24},{17,1},{25,9},{1,17},{9,25},{18,2},{26... | collective-permute-start | bytes 98312 | tf_op jit(solution)/shard_map/ppermute | solution.py:12
  8.3 13.0 %all-to-all-start = ((bf16[8,128,128]{1,2,0:T(8,128)(2,1)}), bf16[8,128,128]{1,2,0:T(8,128)(2,1)}, u32[]{:S(2)}, u32[]{:S(2)}) async-start(bf16[8,128,128]{1,2,0:T(8,128)(2,1)} %broadcast_in_dim.24), calls=%async_computation | async-start | bytes 524288 | tf_op jit(solution)/shard_map/all_to_all | solution.py:36
  23.7 5.7 %collective-permute-start.6 = (f32[2,128]{1,0:T(2,128)S(1)}, f32[2,128]{1,0:T(2,128)S(1)}, u32[]{:S(2)}, u32[]{:S(2)}) collective-permute-start(f32[2,128]{1,0:T(2,128)S(1)} %pad_maximum_fusion), channel_id=1, source_target_pairs={{2,0},{3,1},{4,2},{5,3},{6,4},{7,5},{0,6},{1,7},{10,8},{11,9},{12,... | collective-permute-start | bytes 3080 | tf_op jit(solution)/shard_map/ppermute | solution.py:12
  25.8 7.0 %collective-permute-start.5 = (f32[2,128]{1,0:T(2,128)S(1)}, f32[2,128]{1,0:T(2,128)S(1)}, u32[]{:S(2)}, u32[]{:S(2)}) collective-permute-start(f32[2,128]{1,0:T(2,128)S(1)} %pad_maximum_fusion), channel_id=1, source_target_pairs={{3,0},{4,1},{5,2},{6,3},{7,4},{0,5},{1,6},{2,7},{11,8},{12,9},{13,... | collective-permute-start | bytes 3080 | tf_op jit(solution)/shard_map/ppermute | solution.py:12
  25.8 7.0 %collective-permute-start.4 = (f32[2,128]{1,0:T(2,128)S(1)}, f32[2,128]{1,0:T(2,128)S(1)}, u32[]{:S(2)}, u32[]{:S(2)}) collective-permute-start(f32[2,128]{1,0:T(2,128)S(1)} %pad_maximum_fusion), channel_id=1, source_target_pairs={{4,0},{5,1},{6,2},{7,3},{0,4},{1,5},{2,6},{3,7},{12,8},{13,9},{14,... | collective-permute-start | bytes 3080 | tf_op jit(solution)/shard_map/ppermute | solution.py:12
  28.6 4.2 %collective-permute-start.3 = (f32[2,128]{1,0:T(2,128)S(1)}, f32[2,128]{1,0:T(2,128)S(1)}, u32[]{:S(2)}, u32[]{:S(2)}) collective-permute-start(f32[2,128]{1,0:T(2,128)S(1)} %pad_maximum_fusion), channel_id=1, source_target_pairs={{5,0},{6,1},{7,2},{0,3},{1,4},{2,5},{3,6},{4,7},{13,8},{14,9},{15,... | collective-permute-start | bytes 3080 | tf_op jit(solution)/shard_map/ppermute | solution.py:12
  28.6 4.2 %collective-permute-start.2 = (f32[2,128]{1,0:T(2,128)S(1)}, f32[2,128]{1,0:T(2,128)S(1)}, u32[]{:S(2)}, u32[]{:S(2)}) collective-permute-start(f32[2,128]{1,0:T(2,128)S(1)} %pad_maximum_fusion), channel_id=1, source_target_pairs={{6,0},{7,1},{0,2},{1,3},{2,4},{3,5},{4,6},{5,7},{14,8},{15,9},{8,1... | collective-permute-start | bytes 3080 | tf_op jit(solution)/shard_map/ppermute | solution.py:12
  29.4 4.1 %collective-permute-start.7 = (f32[2,128]{1,0:T(2,128)S(1)}, f32[2,128]{1,0:T(2,128)S(1)}, u32[]{:S(2)}, u32[]{:S(2)}) collective-permute-start(f32[2,128]{1,0:T(2,128)S(1)} %pad_maximum_fusion), channel_id=1, source_target_pairs={{1,0},{2,1},{3,2},{4,3},{5,4},{6,5},{7,6},{0,7},{9,8},{10,9},{11,1... | collective-permute-start | bytes 3080 | tf_op jit(solution)/shard_map/ppermute | solution.py:12
  32.8 5.1 %collective-permute-start.1 = (f32[2,128]{1,0:T(2,128)S(1)}, f32[2,128]{1,0:T(2,128)S(1)}, u32[]{:S(2)}, u32[]{:S(2)}) collective-permute-start(f32[2,128]{1,0:T(2,128)S(1)} %pad_maximum_fusion), channel_id=1, source_target_pairs={{7,0},{0,1},{1,2},{2,3},{3,4},{4,5},{5,6},{6,7},{15,8},{8,9},{9,10... | collective-permute-start | bytes 3080 | tf_op jit(solution)/shard_map/ppermute | solution.py:12
  38.1 11.9 %collective-permute-start.8 = (bf16[1,128,1536]{2,1,0:T(8,128)(2,1)S(1)}, bf16[1,128,1536]{2,1,0:T(8,128)(2,1)S(1)}, u32[]{:S(2)}, u32[]{:S(2)}) collective-permute-start(bf16[1,128,1536]{2,1,0:T(8,128)(2,1)S(1)} %fusion.9), channel_id=1, source_target_pairs={{8,0},{16,8},{24,16},{0,24},{9,1},{17,9},{25,17},{1,25},{10,2},{18... | collective-permute-start | bytes 1179656 | tf_op jit(solution)/shard_map/ppermute | solution.py:12
